TPU v7x, 32 devices: a whole 2x2x4 slice. The times are simulated.
32 devices in a mesh: grp: 2 (over y), tile: 16 (over z, x, core).
Axes of the slice: x: 2, y: 2, z: 4, core: 2. Of those that a mesh axis runs over, the one named last changes fastest.
Arguments:
- level_set: float32 [640, 10240], P('grp', 'tile'), may hold values from -8 to 8
- fuel: int32 [640, 10240], P('grp', 'tile'), may hold values from 0 to 12
- wind: float32 [2, 32, 512], P(None, 'grp', 'tile'), may hold values from -6 to 6
- owner: int32 [2, 16], P('grp'), may hold values from 0 to 15, each once within a row
- active: int32 [4, 2, 16], P(None, 'grp', 'tile'), may hold values 0 or 1
- fuel_rate: float32 [13], replicated, may hold values from 0.05 to 0.3
- fuel_wind: float32 [13], replicated, may hold values from 0.01 to 0.05
- fuel_heat: float32 [13], replicated, may hold values from 0.5 to 4
Outputs:
- level_out: float32 [640, 10240], P('grp', 'tile')
- wind_out: float32 [2, 32, 512], P(None, 'grp', 'tile')
Inputs may be any that keep to these rules, and one draw needn't show every extreme that they name: Each row of owner is a permutation of the 16 tiles of a group.
All inputs are finite; a program needn't handle non-finite values. No bound on the sum of `active` on one device may be relied on, other than what follows from the above.
Results may differ from a plain program's by a relative error of at most 0.0003.
Values sent between devices are 32-bit elements; how exact they have to be, the bound alone decides.
A program may use at most 64 MiB of HBM per device.

v0:
```python
import jax
import jax.numpy as jnp
from jax import lax
from jax.sharding import PartitionSpec as P

STEPS = 2
SUBSTEPS = 2


def extended(shard, sides, width):
    for axis, dim in sides:
        size, length = (lax.axis_size(axis), shard.shape[dim])
        up = [(i, (i + 1) % size) for i in range(size - 1)]
        down = [(j, i) for i, j in up]
        last = lax.slice_in_dim(shard, length - width, length, axis=dim)
        first = lax.slice_in_dim(shard, 0, width, axis=dim)
        before = lax.ppermute(last, axis, up)
        after = lax.ppermute(first, axis, down)
        shard = jnp.concatenate([before, shard, after], axis=dim)
    return shard


def lookup(fuel, table):
    total = jnp.zeros(fuel.shape, jnp.float32)
    for category in range(table.shape[0]):
        total = total + jnp.where(fuel == category, table[category], jnp.float32(0.0))
    return total


def burnt(level):
    return 0.5 * (1.0 - jnp.tanh(level))


def expander(fine_count, coarse_count):
    fine_index = lax.broadcasted_iota(jnp.int32, (fine_count, coarse_count), 0)
    coarse_index = lax.broadcasted_iota(jnp.int32, (fine_count, coarse_count), 1)
    refine = fine_count // coarse_count
    return (fine_index // refine == coarse_index).astype(jnp.float32)


def product(left, right):
    return jnp.dot(left, right, preferred_element_type=jnp.float32, precision=lax.Precision.HIGHEST)


def neighbours(level):
    padded = extended(level, (("grp", 0), ("tile", 1)), 1)
    first_row = lax.axis_index("grp") == 0
    last_row = lax.axis_index("grp") == lax.axis_size("grp") - 1
    first_col = lax.axis_index("tile") == 0
    last_col = lax.axis_index("tile") == lax.axis_size("tile") - 1
    top_edge = jnp.where(first_row, level[0], padded[0, 1:-1])
    bottom_edge = jnp.where(last_row, level[-1], padded[-1, 1:-1])
    left_edge = jnp.where(first_col, level[:, 0], padded[1:-1, 0])
    right_edge = jnp.where(last_col, level[:, -1], padded[1:-1, -1])
    south = jnp.concatenate([top_edge[None, :], level[:-1]], axis=0)
    north_cell = jnp.concatenate([level[1:], bottom_edge[None, :]], axis=0)
    west = jnp.concatenate([left_edge[:, None], level[:, :-1]], axis=1)
    east_cell = jnp.concatenate([level[:, 1:], right_edge[:, None]], axis=1)
    return (south, north_cell, west, east_cell)


def wind_update(block, owned):
    padq = jnp.pad(owned, 1, mode="edge")
    grad_x = (padq[1:-1, 2:] - padq[1:-1, :-2]) * 0.5
    grad_y = (padq[2:, 1:-1] - padq[:-2, 1:-1]) * 0.5
    return jnp.stack([0.9 * block[0] + 40.0 * grad_x, 0.9 * block[1] + 40.0 * grad_y])


def shards(level_set, fuel, wind, owner, active, fuel_rate, fuel_wind, fuel_heat):
    cell_rows, cell_cols = level_set.shape
    atm_rows, atm_cols = (wind.shape[1], wind.shape[2])
    rows_expand = expander(cell_rows, atm_rows)
    cols_expand = expander(cell_cols, atm_cols).T
    rate = lookup(fuel, fuel_rate)
    drift = lookup(fuel, fuel_wind)
    heat = lookup(fuel, fuel_heat)
    owner_row = owner[0]
    myself = lax.axis_index("tile")
    tiles = lax.axis_size("tile")
    slots = jnp.arange(tiles, dtype=jnp.int32)
    readers_of_mine = (owner_row == myself).astype(jnp.float32)
    my_owner = (slots == owner_row[myself]).astype(jnp.float32)
    level = level_set
    counter = 0
    held = wind
    for atmos_step in range(STEPS):
        flat_wind = held.reshape(2 * atm_rows * atm_cols)
        read_everyone = lax.all_gather(flat_wind[None, :], "tile", axis=0, tiled=True)
        got = jnp.sum(my_owner[:, None] * read_everyone, axis=0)
        read_wind = got.reshape(2, atm_rows, atm_cols)
        east = product(product(rows_expand, read_wind[0]), cols_expand)
        north = product(product(rows_expand, read_wind[1]), cols_expand)
        fine_flux = jnp.zeros(level.shape, jnp.float32)
        for substep in range(SUBSTEPS):
            south, north_cell, west, east_cell = neighbours(level)
            back_x = level - west
            ahead_x = east_cell - level
            back_y = level - south
            ahead_y = north_cell - level
            slope = jnp.sqrt(
                jnp.maximum(back_x, 0.0) ** 2
                + jnp.minimum(ahead_x, 0.0) ** 2
                + jnp.maximum(back_y, 0.0) ** 2
                + jnp.minimum(ahead_y, 0.0) ** 2
                + 1e-12
            )
            carry = (
                jnp.maximum(east, 0.0) * back_x
                + jnp.minimum(east, 0.0) * ahead_x
                + jnp.maximum(north, 0.0) * back_y
                + jnp.minimum(north, 0.0) * ahead_y
            )
            candidate = level - rate * slope - drift * carry
            newer = jnp.where(active[counter, 0, 0] > 0, candidate, level)
            fine_flux = fine_flux + heat * (burnt(newer) - burnt(level))
            level = newer
            counter += 1
        refine = cell_rows // atm_rows
        coarse = product(product(rows_expand.T, fine_flux), cols_expand.T) / float(refine * refine)
        flat_flux = coarse.reshape(atm_rows * atm_cols)
        everyone = lax.all_gather(flat_flux[None, :], "tile", axis=0, tiled=True)
        owned = jnp.sum(readers_of_mine[:, None] * everyone, axis=0)
        held = wind_update(held, owned.reshape(atm_rows, atm_cols))
    return (level, held)


def solution(mesh):
    in_specs = (
        P("grp", "tile"),
        P("grp", "tile"),
        P(None, "grp", "tile"),
        P("grp", None),
        P(None, "grp", "tile"),
        P(),
        P(),
        P(),
    )
    out_specs = (P("grp", "tile"), P(None, "grp", "tile"))
    return jax.shard_map(shards, mesh=mesh, in_specs=in_specs, out_specs=out_specs, check_vma=False)
```

profile of v0, /device:TPU:0, one launch (start us, length us, event | category | flops | bytes accessed | tf_op | source)
XLA Modules:
  0.0 204.6 jit_solution(2316475639538666227)
XLA Ops:
  1.4 4.9 %collective-permute-start = (f32[1,640]{1,0:T(1,128)S(1)}, f32[1,640]{1,0:T(1,128)S(1)}, u32[]{:S(2)}, u32[]{:S(2)}) collective-permute-start(f32[1,640]{1,0:T(1,128)S(1)} %get-tuple-element.63), channel_id=1, source_target_pairs={{0,16},{1,17},{2,18},{3,19},{4,20},{5,21},{6,22},{7,23},{8,24},{9,... | collective-permute-start | bytes 7688 | tf_op jit(solution)/shard_map/ppermute | solution.py:17
  7.6 2.9 %fusion.109 = (f32[320,639]{1,0:T(8,128)}, f32[320,639]{1,0:T(8,128)}) fusion(f32[320,640]{1,0:T(8,128)} %param.8), kind=kLoop, calls=%fused_computation.217 | loop fusion | bytes 3271680 | tf_op jit(solution)/shard_map/slice | solution.py:57
  15.3 21.8 %all-gather = f32[16,1,1024]{2,1,0:T(1,128)S(1)} all-gather(f32[1,1,1024]{2,1,0:T(1,128)S(1)} %reshape.88), channel_id=1, replica_groups=mesh['grp'=2,'tile'=16] {'tile'}, dimensions={0}, use_global_device_ids=true | all-gather | bytes 69632 | tf_op jit(solution)/shard_map/all_gather | solution.py:88
  39.5 11.5 %select_add_fusion = (f32[320,640]{1,0:T(8,128)S(1)}, pred[320,640]{1,0:T(32,128)(4,1)S(1)}, pred[320,640]{1,0:T(32,128)(4,1)}, pred[320,640]{1,0:T(32,128)(4,1)...) fusion(f32[]{:T(128)} %bitcast.45, f32[]{:T(128)} %bitcast.44, ...), kind=kLoop, calls=%fused_computation.43 | loop fusion | flops 7782400 | bytes 4300852 | tf_op jit(solution)/shard_map/add | solution.py:26
  54.5 2.4 %collective-permute-start.2 = (f32[322,1]{1,0:T(8,128)S(1)}, f32[322,1]{1,0:T(8,128)S(1)}, u32[]{:S(2)}, u32[]{:S(2)}) collective-permute-start(f32[322,1]{1,0:T(8,128)S(1)} %get-tuple-element.25), channel_id=1, source_target_pairs={{0,1},{1,2},{2,3},{3,4},{4,5},{5,6},{6,7},{7,8},{8,9},{9,10},{10,1... | collective-permute-start | bytes 3872 | tf_op jit(solution)/shard_map/ppermute | solution.py:17
  58.2 2.0 collective-permute-done.3
  60.4 23.2 %subtract_select_fusion.3 = (f32[320,640]{1,0:T(8,128)S(1)}, f32[320,640]{1,0:T(8,128)S(1)}, f32[320,640]{1,0:T(8,128)S(1)}, f32[320,640]{1,0:T(8,128)S(1)}) fusion(f32[320,640]{1,0:T(8,128)S(1)} %copy-done, f32[1,640]{1,0:T(1,128)S(1)} %get-tuple-element.62, f32[319,640]{1,0:T(8,128)} %get-tuple-element.66, f32[319,640]{1,0:T(8,128)} %get-tuple-element.65, ...), kind=kOutput, calls=%fused_computation.45 | convolution fusion | flops 96296960 | bytes 10901225 | tf_op jit(solution)/shard_map/dot_general | solution.py:42
  83.7 4.5 %collective-permute-start.4 = (f32[1,640]{1,0:T(1,128)S(1)}, f32[1,640]{1,0:T(1,128)S(1)}, u32[]{:S(2)}, u32[]{:S(2)}) collective-permute-start(f32[1,640]{1,0:T(1,128)S(1)} %get-tuple-element.53), channel_id=1, source_target_pairs={{0,16},{1,17},{2,18},{3,19},{4,20},{5,21},{6,22},{7,23},{8,24},{9,... | collective-permute-start | bytes 7688 | tf_op jit(solution)/shard_map/ppermute | solution.py:17
  89.8 3.9 %collective-permute-done.5 = f32[1,640]{1,0:T(1,128)S(1)} collective-permute-done((f32[1,640]{1,0:T(1,128)S(1)}, f32[1,640]{1,0:T(1,128)S(1)}, u32[]{:S(2)}, u32[]{:S(2)}) %collective-permute-start.5) | collective-permute-done | bytes 2592 | tf_op jit(solution)/shard_map/ppermute | solution.py:18
  93.8 3.9 %collective-permute-start.6 = (f32[322,1]{1,0:T(8,128)S(1)}, f32[322,1]{1,0:T(8,128)S(1)}, u32[]{:S(2)}, u32[]{:S(2)}) collective-permute-start(f32[322,1]{1,0:T(8,128)S(1)} %get-tuple-element.23), channel_id=1, source_target_pairs={{0,1},{1,2},{2,3},{3,4},{4,5},{5,6},{6,7},{7,8},{8,9},{9,10},{10,1... | collective-permute-start | bytes 3872 | tf_op jit(solution)/shard_map/ppermute | solution.py:17
  97.7 1.5 collective-permute-start.7
  99.2 2.5 %collective-permute-done.7 = f32[322,1]{1,0:T(8,128)S(1)} collective-permute-done((f32[322,1]{1,0:T(8,128)S(1)}, f32[322,1]{1,0:T(8,128)S(1)}, u32[]{:S(2)}, u32[]{:S(2)}) %collective-permute-start.7) | collective-permute-done | bytes 1320 | tf_op jit(solution)/shard_map/ppermute | solution.py:18
  104.6 21.1 %all-gather.1 = f32[16,1,512]{2,1,0:T(1,128)S(1)} all-gather(f32[1,1,512]{2,1,0:T(1,128)S(1)} %reshape.90), channel_id=1, replica_groups=mesh['grp'=2,'tile'=16] {'tile'}, dimensions={0}, use_global_device_ids=true | all-gather | bytes 34816 | tf_op jit(solution)/shard_map/all_gather | solution.py:121
  125.9 1.4 fusion.103
  128.6 1.6 collective-permute-start.8
  131.8 17.3 %all-gather.2 = f32[16,1,1024]{2,1,0:T(1,128)S(1)} all-gather(f32[1,1,1024]{2,1,0:T(1,128)S(1)} %reshape.92), channel_id=1, replica_groups=mesh['grp'=2,'tile'=16] {'tile'}, dimensions={0}, use_global_device_ids=true | all-gather | bytes 69632 | tf_op jit(solution)/shard_map/all_gather | solution.py:88
  151.0 2.4 %collective-permute-start.10 = (f32[322,1]{1,0:T(8,128)S(1)}, f32[322,1]{1,0:T(8,128)S(1)}, u32[]{:S(2)}, u32[]{:S(2)}) collective-permute-start(f32[322,1]{1,0:T(8,128)S(1)} %get-tuple-element.21), channel_id=1, source_target_pairs={{0,1},{1,2},{2,3},{3,4},{4,5},{5,6},{6,7},{7,8},{8,9},{9,10},{10,1... | collective-permute-start | bytes 3872 | tf_op jit(solution)/shard_map/ppermute | solution.py:17
  154.7 3.2 %collective-permute-done.11 = f32[322,1]{1,0:T(8,128)S(1)} collective-permute-done((f32[322,1]{1,0:T(8,128)S(1)}, f32[322,1]{1,0:T(8,128)S(1)}, u32[]{:S(2)}, u32[]{:S(2)}) %collective-permute-start.11) | collective-permute-done | bytes 1320 | tf_op jit(solution)/shard_map/ppermute | solution.py:18
  158.1 2.9 %subtract_select_fusion.1 = (f32[320,640]{1,0:T(8,128)S(1)}, f32[320,640]{1,0:T(8,128)S(1)}) fusion(f32[320,640]{1,0:T(8,128)S(1)} %subtract_select_fusion.2, f32[320,640]{1,0:T(8,128)S(1)} %copy-done.2, f32[320,640]{1,0:T(8,128)S(1)} %get-tuple-element.17, f32[1,640]{1,0:T(1,128)S(1)} %get-tuple-element.42, f32[319,640]{1,0:T(8,128)} %get-tuple-element.46, ...), kind=kOutput, calls=%fused_computation.33 | convolution fusion | flops 86056960 | bytes 8238721 | tf_op jit(solution)/shard_map/dot_general | solution.py:42
  161.1 4.5 %collective-permute-start.12 = (f32[1,640]{1,0:T(1,128)S(1)}, f32[1,640]{1,0:T(1,128)S(1)}, u32[]{:S(2)}, u32[]{:S(2)}) collective-permute-start(f32[1,640]{1,0:T(1,128)S(1)} %get-tuple-element.33), channel_id=1, source_target_pairs={{0,16},{1,17},{2,18},{3,19},{4,20},{5,21},{6,22},{7,23},{8,24},{9,... | collective-permute-start | bytes 7688 | tf_op jit(solution)/shard_map/ppermute | solution.py:17
  167.3 3.9 %collective-permute-done.13 = f32[1,640]{1,0:T(1,128)S(1)} collective-permute-done((f32[1,640]{1,0:T(1,128)S(1)}, f32[1,640]{1,0:T(1,128)S(1)}, u32[]{:S(2)}, u32[]{:S(2)}) %collective-permute-start.13) | collective-permute-done | bytes 2592 | tf_op jit(solution)/shard_map/ppermute | solution.py:18
  171.3 4.4 %collective-permute-start.14 = (f32[322,1]{1,0:T(8,128)S(1)}, f32[322,1]{1,0:T(8,128)S(1)}, u32[]{:S(2)}, u32[]{:S(2)}) collective-permute-start(f32[322,1]{1,0:T(8,128)S(1)} %get-tuple-element.19), channel_id=1, source_target_pairs={{0,1},{1,2},{2,3},{3,4},{4,5},{5,6},{6,7},{7,8},{8,9},{9,10},{10,1... | collective-permute-start | bytes 3872 | tf_op jit(solution)/shard_map/ppermute | solution.py:17
  177.0 2.7 %collective-permute-done.15 = f32[322,1]{1,0:T(8,128)S(1)} collective-permute-done((f32[322,1]{1,0:T(8,128)S(1)}, f32[322,1]{1,0:T(8,128)S(1)}, u32[]{:S(2)}, u32[]{:S(2)}) %collective-permute-start.15) | collective-permute-done | bytes 1320 | tf_op jit(solution)/shard_map/ppermute | solution.py:18
  182.5 21.1 %all-gather.3 = f32[16,1,512]{2,1,0:T(1,128)S(1)} all-gather(f32[1,1,512]{2,1,0:T(1,128)S(1)} %reshape.94), channel_id=1, replica_groups=mesh['grp'=2,'tile'=16] {'tile'}, dimensions={0}, use_global_device_ids=true | all-gather | bytes 34816 | tf_op jit(solution)/shard_map/all_gather | solution.py:121
  (131 shorter events, 29.2 us)
Async XLA Ops:
  1.4 52.9 %collective-permute-start = (f32[1,640]{1,0:T(1,128)S(1)}, f32[1,640]{1,0:T(1,128)S(1)}, u32[]{:S(2)}, u32[]{:S(2)}) collective-permute-start(f32[1,640]{1,0:T(1,128)S(1)} %get-tuple-element.63), channel_id=1, source_target_pairs={{0,16},{1,17},{2,18},{3,19},{4,20},{5,21},{6,22},{7,23},{8,24},{9,... | collective-permute-start | bytes 7688 | tf_op jit(solution)/shard_map/ppermute | solution.py:17
  6.2 48.1 %collective-permute-start.1 = (f32[1,640]{1,0:T(1,128)S(1)}, f32[1,640]{1,0:T(1,128)S(1)}, u32[]{:S(2)}, u32[]{:S(2)}) collective-permute-start(f32[1,640]{1,0:T(1,128)S(1)} %get-tuple-element.64), channel_id=1, source_target_pairs={{16,0},{17,1},{18,2},{19,3},{20,4},{21,5},{22,6},{23,7},{24,8},{25... | collective-permute-start | bytes 7688 | tf_op jit(solution)/shard_map/ppermute | solution.py:18
  13.2 26.3 %copy-start.11 = (s32[320,640]{1,0:T(8,128)S(1)}, s32[320,640]{1,0:T(8,128)}, u32[]{:S(2)}) copy-start(s32[320,640]{1,0:T(8,128)} %param.9) | copy-start | bytes 2457604
  39.5 20.8 %copy-start.3 = (f32[320,640]{1,0:T(8,128)}, f32[320,640]{1,0:T(8,128)S(1)}, u32[]{:S(2)}) copy-start(f32[320,640]{1,0:T(8,128)S(1)} %fusion.29) | copy-start | bytes 2457604
  39.5 11.5 %copy-start.19 = (s32[4,1,1]{0,2,1:T(1,128)S(1)}, s32[4,1,1]{0,2,1:T(1,128)}, u32[]{:S(2)}) copy-start(s32[4,1,1]{0,2,1:T(1,128)} %param.12) | copy-start | bytes 52
  54.5 3.7 %collective-permute-start.2 = (f32[322,1]{1,0:T(8,128)S(1)}, f32[322,1]{1,0:T(8,128)S(1)}, u32[]{:S(2)}, u32[]{:S(2)}) collective-permute-start(f32[322,1]{1,0:T(8,128)S(1)} %get-tuple-element.25), channel_id=1, source_target_pairs={{0,1},{1,2},{2,3},{3,4},{4,5},{5,6},{6,7},{7,8},{8,9},{9,10},{10,1... | collective-permute-start | bytes 3872 | tf_op jit(solution)/shard_map/ppermute | solution.py:17
  56.9 3.3 %collective-permute-start.3 = (f32[322,1]{1,0:T(8,128)S(1)}, f32[322,1]{1,0:T(8,128)S(1)}, u32[]{:S(2)}, u32[]{:S(2)}) collective-permute-start(f32[322,1]{1,0:T(8,128)S(1)} %get-tuple-element.26), channel_id=1, source_target_pairs={{1,0},{2,1},{3,2},{4,3},{5,4},{6,5},{7,6},{8,7},{9,8},{10,9},{11,1... | collective-permute-start | bytes 3872 | tf_op jit(solution)/shard_map/ppermute | solution.py:18
  83.5 18.4 %copy-start.1 = (f32[320,640]{1,0:T(8,128)}, f32[320,640]{1,0:T(8,128)S(1)}, u32[]{:S(2)}) copy-start(f32[320,640]{1,0:T(8,128)S(1)} %get-tuple-element.18) | copy-start | bytes 2457604
  83.7 6.1 %collective-permute-start.4 = (f32[1,640]{1,0:T(1,128)S(1)}, f32[1,640]{1,0:T(1,128)S(1)}, u32[]{:S(2)}, u32[]{:S(2)}) collective-permute-start(f32[1,640]{1,0:T(1,128)S(1)} %get-tuple-element.53), channel_id=1, source_target_pairs={{0,16},{1,17},{2,18},{3,19},{4,20},{5,21},{6,22},{7,23},{8,24},{9,... | collective-permute-start | bytes 7688 | tf_op jit(solution)/shard_map/ppermute | solution.py:17
  88.2 5.5 %collective-permute-start.5 = (f32[1,640]{1,0:T(1,128)S(1)}, f32[1,640]{1,0:T(1,128)S(1)}, u32[]{:S(2)}, u32[]{:S(2)}) collective-permute-start(f32[1,640]{1,0:T(1,128)S(1)} %get-tuple-element.54), channel_id=1, source_target_pairs={{16,0},{17,1},{18,2},{19,3},{20,4},{21,5},{22,6},{23,7},{24,8},{25... | collective-permute-start | bytes 7688 | tf_op jit(solution)/shard_map/ppermute | solution.py:18
  89.8 12.1 %copy-start.4 = (f32[320,640]{1,0:T(8,128)S(1)}, f32[320,640]{1,0:T(8,128)}, u32[]{:S(2)}) copy-start(f32[320,640]{1,0:T(8,128)} %copy-done.3) | copy-start | bytes 2457604
  93.8 5.4 %collective-permute-start.6 = (f32[322,1]{1,0:T(8,128)S(1)}, f32[322,1]{1,0:T(8,128)S(1)}, u32[]{:S(2)}, u32[]{:S(2)}) collective-permute-start(f32[322,1]{1,0:T(8,128)S(1)} %get-tuple-element.23), channel_id=1, source_target_pairs={{0,1},{1,2},{2,3},{3,4},{4,5},{5,6},{6,7},{7,8},{8,9},{9,10},{10,1... | collective-permute-start | bytes 3872 | tf_op jit(solution)/shard_map/ppermute | solution.py:17
  97.7 4.1 %collective-permute-start.7 = (f32[322,1]{1,0:T(8,128)S(1)}, f32[322,1]{1,0:T(8,128)S(1)}, u32[]{:S(2)}, u32[]{:S(2)}) collective-permute-start(f32[322,1]{1,0:T(8,128)S(1)} %get-tuple-element.24), channel_id=1, source_target_pairs={{1,0},{2,1},{3,2},{4,3},{5,4},{6,5},{7,6},{8,7},{9,8},{10,9},{11,1... | collective-permute-start | bytes 3872 | tf_op jit(solution)/shard_map/ppermute | solution.py:18
  128.6 22.3 %collective-permute-start.8 = (f32[1,640]{1,0:T(1,128)S(1)}, f32[1,640]{1,0:T(1,128)S(1)}, u32[]{:S(2)}, u32[]{:S(2)}) collective-permute-start(f32[1,640]{1,0:T(1,128)S(1)} %get-tuple-element.43), channel_id=1, source_target_pairs={{0,16},{1,17},{2,18},{3,19},{4,20},{5,21},{6,22},{7,23},{8,24},{9,... | collective-permute-start | bytes 7688 | tf_op jit(solution)/shard_map/ppermute | solution.py:17
  130.2 20.7 %collective-permute-start.9 = (f32[1,640]{1,0:T(1,128)S(1)}, f32[1,640]{1,0:T(1,128)S(1)}, u32[]{:S(2)}, u32[]{:S(2)}) collective-permute-start(f32[1,640]{1,0:T(1,128)S(1)} %get-tuple-element.44), channel_id=1, source_target_pairs={{16,0},{17,1},{18,2},{19,3},{20,4},{21,5},{22,6},{23,7},{24,8},{25... | collective-permute-start | bytes 7688 | tf_op jit(solution)/shard_map/ppermute | solution.py:18
  149.7 8.3 %copy-start.9 = (f32[320,639]{1,0:T(8,128)S(1)}, f32[320,639]{1,0:T(8,128)}, u32[]{:S(2)}) copy-start(f32[320,639]{1,0:T(8,128)} %get-tuple-element.40) | copy-start | bytes 2453764
  149.7 8.3 %copy-start.10 = (f32[319,640]{1,0:T(8,128)S(1)}, f32[319,640]{1,0:T(8,128)}, u32[]{:S(2)}) copy-start(f32[319,640]{1,0:T(8,128)} %get-tuple-element.45) | copy-start | bytes 2449924
  150.9 7.2 %copy-start.2 = (f32[320,640]{1,0:T(8,128)S(1)}, f32[320,640]{1,0:T(8,128)}, u32[]{:S(2)}) copy-start(f32[320,640]{1,0:T(8,128)} %copy-done.1) | copy-start | bytes 2457604
  151.0 3.7 %collective-permute-start.10 = (f32[322,1]{1,0:T(8,128)S(1)}, f32[322,1]{1,0:T(8,128)S(1)}, u32[]{:S(2)}, u32[]{:S(2)}) collective-permute-start(f32[322,1]{1,0:T(8,128)S(1)} %get-tuple-element.21), channel_id=1, source_target_pairs={{0,1},{1,2},{2,3},{3,4},{4,5},{5,6},{6,7},{7,8},{8,9},{9,10},{10,1... | collective-permute-start | bytes 3872 | tf_op jit(solution)/shard_map/ppermute | solution.py:17
  153.4 4.5 %collective-permute-start.11 = (f32[322,1]{1,0:T(8,128)S(1)}, f32[322,1]{1,0:T(8,128)S(1)}, u32[]{:S(2)}, u32[]{:S(2)}) collective-permute-start(f32[322,1]{1,0:T(8,128)S(1)} %get-tuple-element.22), channel_id=1, source_target_pairs={{1,0},{2,1},{3,2},{4,3},{5,4},{6,5},{7,6},{8,7},{9,8},{10,9},{11,1... | collective-permute-start | bytes 3872 | tf_op jit(solution)/shard_map/ppermute | solution.py:18
  161.1 6.1 %collective-permute-start.12 = (f32[1,640]{1,0:T(1,128)S(1)}, f32[1,640]{1,0:T(1,128)S(1)}, u32[]{:S(2)}, u32[]{:S(2)}) collective-permute-start(f32[1,640]{1,0:T(1,128)S(1)} %get-tuple-element.33), channel_id=1, source_target_pairs={{0,16},{1,17},{2,18},{3,19},{4,20},{5,21},{6,22},{7,23},{8,24},{9,... | collective-permute-start | bytes 7688 | tf_op jit(solution)/shard_map/ppermute | solution.py:17
  165.7 5.5 %collective-permute-start.13 = (f32[1,640]{1,0:T(1,128)S(1)}, f32[1,640]{1,0:T(1,128)S(1)}, u32[]{:S(2)}, u32[]{:S(2)}) collective-permute-start(f32[1,640]{1,0:T(1,128)S(1)} %get-tuple-element.34), channel_id=1, source_target_pairs={{16,0},{17,1},{18,2},{19,3},{20,4},{21,5},{22,6},{23,7},{24,8},{25... | collective-permute-start | bytes 7688 | tf_op jit(solution)/shard_map/ppermute | solution.py:18
  171.3 5.7 %collective-permute-start.14 = (f32[322,1]{1,0:T(8,128)S(1)}, f32[322,1]{1,0:T(8,128)S(1)}, u32[]{:S(2)}, u32[]{:S(2)}) collective-permute-start(f32[322,1]{1,0:T(8,128)S(1)} %get-tuple-element.19), channel_id=1, source_target_pairs={{0,1},{1,2},{2,3},{3,4},{4,5},{5,6},{6,7},{7,8},{8,9},{9,10},{10,1... | collective-permute-start | bytes 3872 | tf_op jit(solution)/shard_map/ppermute | solution.py:17
  175.7 4.1 %collective-permute-start.15 = (f32[322,1]{1,0:T(8,128)S(1)}, f32[322,1]{1,0:T(8,128)S(1)}, u32[]{:S(2)}, u32[]{:S(2)}) collective-permute-start(f32[322,1]{1,0:T(8,128)S(1)} %get-tuple-element.20), channel_id=1, source_target_pairs={{1,0},{2,1},{3,2},{4,3},{5,4},{6,5},{7,6},{8,7},{9,8},{10,9},{11,1... | collective-permute-start | bytes 3872 | tf_op jit(solution)/shard_map/ppermute | solution.py:18
  (13 other events, 49.6 us)
where the time goes:
time: 206 us; the launch traced here: 205 us
  blocking collectives  81.2 us (39%)
  starting transfers between devices  39.1 us (19%)
  matrix products  32.4 us (16%)
  waiting for transfers between devices  18.3 us (9%)
  other arithmetic  16.7 us (8%)
  local copies, waits for them, and re-layouts  12.9 us (6%)
  between operations  3.98 us (2%)
    all_gather x2, blocking collectives, shards(): everyone = lax.all_gather(flat_flux[None, :], 'tile', axis=0, tiled=True)  42.1 us
    all_gather x2, blocking collectives, shards(): lax.all_gather(flat_wind[None, :], 'tile', axis=0, tiled=True)  39.1 us
    dot_general x12, matrix products, product(): jnp.dot(left, right, preferred_element_type=jnp.float32, precision=lax.Pr...  32.4 us
    ppermute x8, starting transfers between devices, extended(): before = lax.ppermute(last, axis, up)  28.6 us
    ppermute x8, waiting for transfers between devices, extended(): after = lax.ppermute(first, axis, down)  18.2 us
    add x1, other arithmetic, lookup(): total + jnp.where(fuel == category, table[category], jnp.float32(0.0))  11.5 us
    ppermute x8, starting transfers between devices, extended(): after = lax.ppermute(first, axis, down)  10.5 us
    slice x4, local copies, waits for them, and re-layouts, neighbours(): west = jnp.concatenate([left_edge[:, None], level[:, :-1]], axis=1)  4.9 us
  transfers between devices with their start and end apart: 16, of which 6 were waited for; matrix products, arithmetic and copies ran while one was open for 12% of the time, Pallas kernels for 0%

commit v1 on v0

v1 whole, which is shorter than its diff:
```python
import functools

import jax
import jax.numpy as jnp
from jax import lax
from jax.experimental import pallas as pl
from jax.experimental.pallas import tpu as pltpu
from jax.sharding import PartitionSpec as P

STEPS = 2
SUBSTEPS = 2
SUBS = STEPS * SUBSTEPS
MESH = pl.DeviceIdType.MESH
LANES = 128
ROWS = 8
F32 = jnp.float32
BF16 = jnp.bfloat16


def thirds(x):
    high = x.astype(BF16)
    rest = x - high.astype(F32)
    middle = rest.astype(BF16)
    low = (rest - middle.astype(F32)).astype(BF16)
    return [high, middle, low]


def exact_dots(arrays, right):
    pieces = [piece for x in arrays for piece in thirds(x)]
    full = jnp.dot(jnp.concatenate(pieces, axis=0), right, preferred_element_type=F32)
    m = arrays[0].shape[0]
    return [
        full[3 * i * m : (3 * i + 1) * m] + full[(3 * i + 1) * m : (3 * i + 2) * m] + full[(3 * i + 2) * m : (3 * i + 3) * m]
        for i in range(len(arrays))
    ]


def kernel(
    grps, tiles, atm_rows, atm_cols,
    level_ref, fuel_ref, wind_ref, owner_ref, active_ref, rate_tab, wind_tab, heat_tab,
    level_out, wind_out,
    lev_a, lev_b, fuel, rate, drift, heat, burn, row_sums, gust, spread, gather_cols,
    send, halo, wind_first, wind_last, slots_first, slots_last,
    load_sem, send_sem, recv_sem, wind_sem, out_sem,
):
    cell_rows, cell_cols = fuel.shape
    refine = cell_rows // atm_rows
    cols = cell_cols // LANES
    group = 2 * refine
    tiles_in = group // ROWS
    groups = cell_rows // group
    g, t = lax.axis_index("grp"), lax.axis_index("tile")

    load_level = [
        pltpu.make_async_copy(
            level_ref.at[:, pl.ds(c * LANES, LANES)], lev_a.at[c, pl.ds(ROWS, cell_rows), :], load_sem.at[c]
        )
        for c in range(cols)
    ]
    load_fuel = pltpu.make_async_copy(fuel_ref, fuel, load_sem.at[cols])
    outer, inner = (0, cols - 1), tuple(range(1, cols - 1))
    for c in outer + inner:
        load_level[c].start()
    load_fuel.start()

    barrier = pltpu.get_barrier_semaphore()
    for d in range(1, tiles):
        pl.semaphore_signal(barrier, inc=1, device_id=(g, lax.rem(t + d, tiles)), device_id_type=MESH)

    @pl.when(g > 0)
    def _():
        pl.semaphore_signal(barrier, inc=1, device_id=(g - 1, t), device_id_type=MESH)

    @pl.when(g < grps - 1)
    def _():
        pl.semaphore_signal(barrier, inc=1, device_id=(g + 1, t), device_id_type=MESH)

    lane = lax.broadcasted_iota(jnp.int32, (ROWS, LANES), 1)
    sub = lax.broadcasted_iota(jnp.int32, (ROWS, LANES), 0)
    lane16 = lax.broadcasted_iota(jnp.int32, (atm_rows, LANES), 1)
    sub16 = lax.broadcasted_iota(jnp.int32, (atm_rows, LANES), 0)
    quarter = atm_cols

    def pack(east, north):
        top, low = slice(0, ROWS), slice(ROWS, 2 * ROWS)
        return jnp.where(
            lane < quarter, east[top],
            jnp.where(
                lane < 2 * quarter, pltpu.roll(east[low], quarter, 1),
                jnp.where(lane < 3 * quarter, pltpu.roll(north[top], 2 * quarter, 1), pltpu.roll(north[low], 3 * quarter, 1)),
            ),
        )

    def unpack(packed):
        east = jnp.concatenate([packed, pltpu.roll(packed, 3 * quarter, 1)], axis=0)
        north = jnp.concatenate([pltpu.roll(packed, 2 * quarter, 1), pltpu.roll(packed, quarter, 1)], axis=0)
        return east, north

    def share(packed, source, slots, index):
        source[...] = packed
        slots[t] = packed
        for d in range(1, tiles):
            pltpu.make_async_remote_copy(
                src_ref=source, dst_ref=slots.at[t],
                send_sem=wind_sem.at[2 * index], recv_sem=wind_sem.at[2 * index + 1],
                device_id=(g, lax.rem(t + d, tiles)), device_id_type=MESH,
            ).start()

    def await_all(slots, sem):
        others = slots.at[pl.ds(0, tiles - 1)]
        pltpu.make_async_copy(others, others, sem).wait()

    def halo_copy(k, side, there):
        return pltpu.make_async_remote_copy(
            src_ref=send.at[k, side], dst_ref=halo.at[k, side],
            send_sem=send_sem.at[k, side], recv_sem=recv_sem.at[k, side],
            device_id=there, device_id_type=MESH,
        )

    going = (t < tiles - 1, t > 0, g < grps - 1, g > 0)
    coming = (t > 0, t < tiles - 1, g > 0, g < grps - 1)
    targets = ((g, t + 1), (g, t - 1), (g + 1, t), (g - 1, t))

    def start_sides(k, sides):
        for side in sides:
            @pl.when(going[side])
            def _(side=side):
                halo_copy(k, side, targets[side]).start()

            @pl.when(jnp.logical_not(coming[side]))
            def _(side=side):
                halo[k, side] = send[k, side ^ 1]

    def wait_sides(k):
        for side in range(4):
            @pl.when(coming[side])
            def _(side=side):
                halo_copy(k, side, targets[side ^ 1]).wait_recv()

    def start_columns(k, west_col, east_col):
        send[k, 1] = west_col
        send[k, 0] = east_col
        start_sides(k, (0, 1))

    def start_rows(k, level):
        for side, row in ((2, ROWS + cell_rows - 1), (3, ROWS)):
            send[k, side] = jnp.zeros((ROWS, LANES), F32)
            for c in range(cols):
                send[k, side, c : c + 1, :] = level[c, row : row + 1, :]
        start_sides(k, (2, 3))

    def place_rows(k, level):
        for side, row in ((2, ROWS - 1), (3, ROWS + cell_rows)):
            for c in range(cols):
                level[c, row : row + 1, :] = halo[k, side, c : c + 1, :]

    def columns_into(packs, k, first, last):
        west_pack, east_pack = packs
        west_pack = jnp.where(lane == k, pltpu.roll(first, k, 1), west_pack)
        east_pack = jnp.where(lane == k, pltpu.roll(last, k + 1, 1), east_pack)
        return west_pack, east_pack

    blank = jnp.zeros((atm_rows, LANES - atm_cols), F32)
    mine = [jnp.concatenate([wind_ref[i], blank], axis=1) for i in range(2)]
    packed_wind = pack(mine[0], mine[1])
    for c in outer:
        load_level[c].wait()

    def first_columns(i, packs):
        for q in range(tiles_in):
            k = i * tiles_in + q
            rows = pl.ds(pl.multiple_of(ROWS + k * ROWS, ROWS), ROWS)
            packs = columns_into(packs, k, lev_a[0, rows, :], lev_a[cols - 1, rows, :])
        return packs

    empty = jnp.zeros((ROWS, LANES), F32)
    packs = lax.fori_loop(0, groups, first_columns, (empty, empty))
    pl.semaphore_wait(barrier, tiles - 1 + (g > 0).astype(jnp.int32) + (g < grps - 1).astype(jnp.int32))
    share(packed_wind, wind_first, slots_first, 0)
    start_columns(0, *packs)
    for c in inner:
        load_level[c].wait()
    start_rows(0, lev_a)

    index = lax.broadcasted_iota(jnp.int32, spread.shape, 0) * refine
    place = lax.broadcasted_iota(jnp.int32, spread.shape, 1)
    spread[...] = jnp.where((place >= index) & (place < index + refine), 1.0, 0.0).astype(BF16)
    index = lax.broadcasted_iota(jnp.int32, gather_cols.shape, 1) * refine
    place = lax.broadcasted_iota(jnp.int32, gather_cols.shape, 0)
    gather_cols[...] = jnp.where((place >= index) & (place < index + refine), 1.0, 0.0).astype(BF16)

    def table(ref):
        values = jnp.zeros((ROWS, LANES), F32)
        for category in range(ref.shape[0]):
            values = jnp.where(lane == category, ref[category], values)
        return values

    tables = [table(ref) for ref in (rate_tab, wind_tab, heat_tab)]
    load_fuel.wait()

    def prepare(i, carry):
        for q in range(tiles_in):
            start = pl.multiple_of((i * tiles_in + q) * ROWS, ROWS)
            rows = pl.ds(start, ROWS)
            for c in range(cols):
                at = slice(c * LANES, (c + 1) * LANES)
                category = fuel[rows, at]
                for values, out in zip(tables, (rate, drift, heat)):
                    out[rows, at] = jnp.take_along_axis(values, category, axis=1, mode="promise_in_bounds")
                burn[rows, at] = jnp.tanh(lev_a[c, pl.ds(pl.multiple_of(start + ROWS, ROWS), ROWS), :])
        return carry

    lax.fori_loop(0, groups, prepare, 0)

    def expand(east, north):
        wide = exact_dots([east, north], spread[...])
        for part in range(2):
            for c in range(cols):
                gust[part, c] = wide[part][:, c * LANES : (c + 1) * LANES]

    await_all(slots_first, wind_sem.at[1])
    east, north = unpack(slots_first[owner_ref[0, t]])
    expand(east, north)

    def block(i, k, src, dst, want, packs):
        flux = k % SUBSTEPS == SUBSTEPS - 1
        burning = jnp.where(active_ref[k, 0, 0] > 0, F32(1.0), F32(0.0))
        ends = 0 in want
        if ends:
            west_halo, east_halo = halo[k, 0], halo[k, 1]
        around = sorted({n for c in want for n in (c - 1, c, c + 1) if 0 <= n < cols})
        winds = {}
        for c in want:
            winds[c] = [
                [jnp.broadcast_to(gust[part, c, pl.ds(2 * i + a, 1), :], (ROWS, LANES)) for a in range(2)] for part in range(2)
            ]
        sums = {c: [None, None] for c in want}

        def add(c, a, x):
            sums[c][a] = x if sums[c][a] is None else sums[c][a] + x

        for q in range(tiles_in):
            kk = i * tiles_in + q
            start = pl.multiple_of(kk * ROWS, ROWS)
            rows, padded = pl.ds(start, ROWS), pl.ds(pl.multiple_of(start + ROWS, ROWS), ROWS)
            here = {c: src[c, padded, :] for c in around}
            right = {c: pltpu.roll(here[c], 1, 1) for c in around if c in want or c + 1 in want}
            left = {c: pltpu.roll(here[c], LANES - 1, 1) for c in around if c in want or c - 1 in want}
            if ends:
                right[-1] = pltpu.roll(west_halo, lax.rem(LANES - kk, LANES), 1)
                left[cols] = pltpu.roll(east_halo, LANES - 1 - kk, 1)
            low, high = (q * ROWS) // refine, (q * ROWS + ROWS - 1) // refine
            split = refine * high - q * ROWS
            new_edge = {}
            for c in want:
                at = slice(c * LANES, (c + 1) * LANES)
                level = here[c]
                above = src[c, pl.ds(start + ROWS - 1, ROWS), :]
                below = src[c, pl.ds(start + ROWS + 1, ROWS), :]
                back_x = level - jnp.where(lane == 0, right[c - 1], right[c])
                ahead_x = jnp.where(lane == LANES - 1, left[c + 1], left[c]) - level
                back_y = level - above
                ahead_y = below - level
                square = (
                    jnp.maximum(back_x, 0.0) ** 2 + jnp.minimum(ahead_x, 0.0) ** 2
                    + jnp.maximum(back_y, 0.0) ** 2 + jnp.minimum(ahead_y, 0.0) ** 2 + 1e-12
                )
                slope = square * lax.rsqrt(square)
                if low == high:
                    east_w, north_w = winds[c][0][low], winds[c][1][low]
                else:
                    east_w = jnp.where(sub < split, winds[c][0][low], winds[c][0][high])
                    north_w = jnp.where(sub < split, winds[c][1][low], winds[c][1][high])
                carry = east_w * jnp.where(east_w > 0.0, back_x, ahead_x) + north_w * jnp.where(north_w > 0.0, back_y, ahead_y)
                newer = level - burning * (rate[rows, at] * slope + drift[rows, at] * carry)
                dst[c, padded, :] = newer
                new_edge[c] = newer
                if flux:
                    now = jnp.tanh(newer)
                    released = heat[rows, at] * (burn[rows, at] - now)
                    if k < SUBS - 1:
                        burn[rows, at] = now
                    if low == high:
                        add(c, low, released)
                    else:
                        add(c, low, jnp.where(sub < split, released, 0.0))
                        add(c, high, jnp.where(sub < split, 0.0, released))
            if ends and k < SUBS - 1:
                packs = columns_into(packs, kk, new_edge[0], new_edge[cols - 1])
        if flux:
            for c in want:
                for a in range(2):
                    row_sums[c, pl.ds(2 * i + a, 1), :] = jnp.sum(sums[c][a], axis=0, keepdims=True)
        return packs

    buffers = (lev_a, lev_b)
    store_level = [
        pltpu.make_async_copy(
            buffers[SUBS % 2].at[c, pl.ds(ROWS, cell_rows), :], level_out.at[:, pl.ds(c * LANES, LANES)], out_sem.at[c]
        )
        for c in range(cols)
    ]
    for k in range(SUBS):
        src, dst = buffers[k % 2], buffers[(k + 1) % 2]
        wait_sides(k)
        place_rows(k, src)
        packs = lax.fori_loop(0, groups, lambda i, p: block(i, k, src, dst, outer, p), (empty, empty))
        if k < SUBS - 1:
            start_columns(k + 1, *packs)
        else:
            for c in outer:
                store_level[c].start()

        def middle(i, carry):
            block(i, k, src, dst, inner, None)
            return carry

        lax.fori_loop(0, 2, lambda n, carry: middle(n * (groups - 1), carry), 0)
        if k < SUBS - 1:
            start_rows(k + 1, dst)
        lax.fori_loop(1, groups - 1, middle, 0)
        if k == SUBS - 1:
            for c in inner:
                store_level[c].start()
        if k % SUBSTEPS == SUBSTEPS - 1:
            coarse = exact_dots([jnp.concatenate([row_sums[c] for c in range(cols)], axis=1)], gather_cols[...])[0] * F32(0.5 / (refine * refine))
            west = jnp.where(lane16 == 0, coarse, pltpu.roll(coarse, 1, 1))
            east_c = jnp.where(lane16 == atm_cols - 1, coarse, pltpu.roll(coarse, LANES - 1, 1))
            up = jnp.where(sub16 == 0, coarse, pltpu.roll(coarse, 1, 0))
            down = jnp.where(sub16 == atm_rows - 1, coarse, pltpu.roll(coarse, atm_rows - 1, 0))
            east = 0.9 * east + 40.0 * ((east_c - west) * 0.5)
            north = 0.9 * north + 40.0 * ((down - up) * 0.5)
            if k < SUBS - 1:
                expand(east, north)

    share(pack(east, north), wind_last, slots_last, 1)
    source = jnp.int32(0)
    for j in range(tiles):
        source = jnp.where(owner_ref[0, j] == t, jnp.int32(j), source)
    await_all(slots_last, wind_sem.at[3])
    east, north = unpack(slots_last[source])
    wind_out[0] = east[:, :atm_cols]
    wind_out[1] = north[:, :atm_cols]
    for copy in store_level:
        copy.wait()
    await_all(slots_first, wind_sem.at[0])
    await_all(slots_last, wind_sem.at[2])
    for k in range(SUBS):
        for side in range(4):
            @pl.when(going[side])
            def _(k=k, side=side):
                halo_copy(k, side, targets[side]).wait_send()


def shards(grps, tiles, level_set, fuel, wind, owner, active, fuel_rate, fuel_wind, fuel_heat):
    cell_rows, cell_cols = level_set.shape
    atm_rows, atm_cols = wind.shape[1], wind.shape[2]
    cells = pltpu.VMEM((cell_rows, cell_cols), F32)
    cols = cell_cols // LANES
    padded = pltpu.VMEM((cols, cell_rows + 2 * ROWS, LANES), F32)
    tile = (ROWS, LANES)
    vmem, smem = pl.BlockSpec(memory_space=pltpu.VMEM), pl.BlockSpec(memory_space=pltpu.SMEM)
    anywhere = pl.BlockSpec(memory_space=pl.ANY)
    return pl.pallas_call(
        functools.partial(kernel, grps, tiles, atm_rows, atm_cols),
        out_shape=(jax.ShapeDtypeStruct(level_set.shape, F32), jax.ShapeDtypeStruct(wind.shape, F32)),
        in_specs=[anywhere, anywhere, vmem, smem, smem, smem, smem, smem],
        out_specs=(anywhere, vmem),
        scratch_shapes=[
            padded, padded,
            pltpu.VMEM((cell_rows, cell_cols), jnp.int32),
            cells, cells, cells, cells,
            pltpu.VMEM((cols, atm_rows, LANES), F32),
            pltpu.VMEM((2, cols, atm_rows, LANES), F32),
            pltpu.VMEM((LANES, cell_cols), BF16),
            pltpu.VMEM((cell_cols, LANES), BF16),
            pltpu.VMEM((SUBS, 4) + tile, F32),
            pltpu.VMEM((SUBS, 4) + tile, F32),
            pltpu.VMEM(tile, F32),
            pltpu.VMEM(tile, F32),
            pltpu.VMEM((tiles,) + tile, F32),
            pltpu.VMEM((tiles,) + tile, F32),
            pltpu.SemaphoreType.DMA((cols + 1,)),
            pltpu.SemaphoreType.DMA((SUBS, 4)),
            pltpu.SemaphoreType.DMA((SUBS, 4)),
            pltpu.SemaphoreType.DMA((4,)),
            pltpu.SemaphoreType.DMA((cols,)),
        ],
        compiler_params=pltpu.CompilerParams(
            collective_id=0, has_side_effects=True, vmem_limit_bytes=32 * 1024 * 1024
        ),
    )(level_set, fuel, wind, owner, active, fuel_rate, fuel_wind, fuel_heat)


def solution(mesh):
    in_specs = (
        P("grp", "tile"),
        P("grp", "tile"),
        P(None, "grp", "tile"),
        P("grp", None),
        P(None, "grp", "tile"),
        P(),
        P(),
        P(),
    )
    out_specs = (P("grp", "tile"), P(None, "grp", "tile"))
    body = functools.partial(shards, mesh.shape["grp"], mesh.shape["tile"])
    return jax.shard_map(body, mesh=mesh, in_specs=in_specs, out_specs=out_specs, check_vma=False)
```

time: 206 us -> 38.8 us (0.19)
  blocking collectives: 81.2 us -> 0 us
  starting transfers between devices: 39.1 us -> 0 us
  Pallas kernels: 0 us -> 32.5 us
  matrix products: 32.4 us -> 0 us
  waiting for transfers between devices: 18.3 us -> 0 us
  other arithmetic: 16.7 us -> 0 us
  local copies, waits for them, and re-layouts: 12.9 us -> 5.28 us
  between operations: 3.98 us -> 0.69 us
    all_gather x4 -> x0, blocking collectives: 81.2 us -> none  [the longest x2 42.1 us: shards(): everyone = lax.all_gather(flat_flux[None, :], 'tile', axis=0, tiled=True)]
    ppermute x16 -> x0, starting transfers between devices: 39.1 us -> none  [the longest x8 28.6 us: extended(): before = lax.ppermute(last, axis, up)]
    pallas_call x0 -> x1, Pallas kernels: none -> 32.5 us  [shards(): pl.pallas_call(functools.partial(kernel, grps, tiles, atm_rows, atm_cols)...]
    dot_general x12 -> x0, matrix products: 32.4 us -> none  [product(): jnp.dot(left, right, preferred_element_type=jnp.float32, precision=lax.Pr...]
    ppermute x16 -> x0, waiting for transfers between devices: 18.3 us -> none  [the longest x8 18.2 us: extended(): after = lax.ppermute(first, axis, down)]
    add x2 -> x0, other arithmetic: 11.6 us -> none  [the longest x1 11.5 us: lookup(): total + jnp.where(fuel == category, table[category], jnp.float32(0.0))]
    slice x22 -> x0, local copies, waits for them, and re-layouts: 11.5 us -> none  [the longest x4 4.9 us: neighbours(): west = jnp.concatenate([left_edge[:, None], level[:, :-1]], axis=1)]
    unnamed x46 -> x17, local copies, waits for them, and re-layouts: 0.42 us -> 5.28 us
  transfers between devices with their start and end apart: 16 -> 0, of which waited for: 6 -> 0; matrix products, arithmetic and copies ran while one was open for 12% -> 0% of each run, Pallas kernels for 0% -> 0%
where the time goes in v1:
time: 38.8 us; the launch traced here: 38.5 us
  Pallas kernels  32.5 us (84%)
  local copies, waits for them, and re-layouts  5.28 us (14%)
  between operations  0.69 us (2%)
    pallas_call x1, Pallas kernels, shards(): pl.pallas_call(functools.partial(kernel, grps, tiles, atm_rows, atm_cols)...  32.5 us
    unnamed x17, local copies, waits for them, and re-layouts  5.28 us

profile of v1, /device:TPU:0, one launch (start us, length us, event | category | flops | bytes accessed | tf_op | source)
XLA Modules:
  0.0 38.5 jit_solution(10065265478924085579)
XLA Ops:
  0.6 0.0 copy-start.6
  0.6 0.0 copy-start.5
  0.7 0.0 copy-start.4
  0.7 0.0 copy-start.3
  0.7 0.8 %copy.10.active_ref = s32[4,1,1]{2,1,0:T(1,128)S(1)} copy(s32[4,1,1]{0,2,1:T(1,128)} %param.12) | data formatting | bytes 32 | tf_op args[4]
  1.4 0.0 copy-done.6
  1.4 0.0 copy-done.5
  1.4 0.0 copy-done.4
  1.4 0.0 copy-done.3
  1.5 0.0 copy-start
  1.5 1.1 %copy-done = f32[320,640]{1,0:T(8,128)S(1)} copy-done((f32[320,640]{1,0:T(8,128)S(1)}, f32[320,640]{1,0:T(8,128)}, u32[]{:S(2)}) %copy-start) | copy-done | bytes 819224
  2.6 0.0 copy-start.1
  2.6 1.1 %copy-done.1 = s32[320,640]{1,0:T(8,128)S(1)} copy-done((s32[320,640]{1,0:T(8,128)S(1)}, s32[320,640]{1,0:T(8,128)}, u32[]{:S(2)}) %copy-start.1) | copy-done | bytes 819224
  3.7 0.0 copy-start.2
  3.7 0.7 %copy-done.2 = f32[2,16,32]{2,1,0:T(8,128)S(1)} copy-done((f32[2,16,32]{2,1,0:T(8,128)S(1)}, f32[2,16,32]{2,1,0:T(8,128)}, u32[]{:S(2)}) %copy-start.2) | copy-done | bytes 4120
  4.5 32.5 %shard_map.95 = (f32[320,640]{1,0:T(8,128)S(1)}, f32[2,16,32]{2,1,0:T(8,128)S(1)}) custom-call(f32[320,640]{1,0:T(8,128)S(1)} %copy-done, s32[320,640]{1,0:T(8,128)S(1)} %copy-done.1, f32[2,16,32]{2,1,0:T(8,128)S(1)} %copy-done.2, s32[1,16]{1,0:T(1,128)S(1)} %copy-done.3, s32[4,1,1]{2,1,0:T(1,128)S(1)} %copy.10.active_ref, f32[13]{0:T(128)S(1)} %copy-done.4, ...), custom_call_target="tpu_custom_call" | custom-call | tf_op jit(solution)/shard_map/pallas_call | solution.py:364
  37.0 0.9 %copy.13 = f32[320,640]{1,0:T(8,128)} copy(f32[320,640]{1,0:T(8,128)S(1)} %get-tuple-element.4) | data formatting | bytes 1638400
  37.9 0.6 %copy.14 = f32[2,16,32]{2,1,0:T(8,128)} copy(f32[2,16,32]{2,1,0:T(8,128)S(1)} %get-tuple-element.5) | data formatting | bytes 8192
Async XLA Ops:
  0.6 0.8 %copy-start.6 = (f32[13]{0:T(128)S(1)}, f32[13]{0:T(128)}, u32[]{:S(2)}) copy-start(f32[13]{0:T(128)} %heat_tab.1) | copy-start | bytes 160
  0.6 0.8 %copy-start.5 = (f32[13]{0:T(128)S(1)}, f32[13]{0:T(128)}, u32[]{:S(2)}) copy-start(f32[13]{0:T(128)} %wind_tab.1) | copy-start | bytes 160
  0.7 0.8 %copy-start.4 = (f32[13]{0:T(128)S(1)}, f32[13]{0:T(128)}, u32[]{:S(2)}) copy-start(f32[13]{0:T(128)} %rate_tab.1) | copy-start | bytes 160
  0.7 0.8 %copy-start.3 = (s32[1,16]{1,0:T(1,128)S(1)}, s32[1,16]{1,0:T(1,128)}, u32[]{:S(2)}) copy-start(s32[1,16]{1,0:T(1,128)} %owner_ref.1) | copy-start | bytes 196
  1.5 1.1 %copy-start = (f32[320,640]{1,0:T(8,128)S(1)}, f32[320,640]{1,0:T(8,128)}, u32[]{:S(2)}) copy-start(f32[320,640]{1,0:T(8,128)} %level_ref.1) | copy-start | bytes 2457604
  2.6 1.1 %copy-start.1 = (s32[320,640]{1,0:T(8,128)S(1)}, s32[320,640]{1,0:T(8,128)}, u32[]{:S(2)}) copy-start(s32[320,640]{1,0:T(8,128)} %fuel_ref.1) | copy-start | bytes 2457604
  3.7 0.7 %copy-start.2 = (f32[2,16,32]{2,1,0:T(8,128)S(1)}, f32[2,16,32]{2,1,0:T(8,128)}, u32[]{:S(2)}) copy-start(f32[2,16,32]{2,1,0:T(8,128)} %wind_ref.1) | copy-start | bytes 12292

commit v2 on v1

--- a/solution.py
+++ b/solution.py
@@ -37,11 +37,12 @@
 
 def kernel(
     grps, tiles, atm_rows, atm_cols,
-    level_ref, fuel_ref, wind_ref, owner_ref, active_ref, rate_tab, wind_tab, heat_tab,
+    level_ref, fuel_ref, wind_any, owner_any, active_any, rate_any, drift_any, heat_any,
     level_out, wind_out,
     lev_a, lev_b, fuel, rate, drift, heat, burn, row_sums, gust, spread, gather_cols,
     send, halo, wind_first, wind_last, slots_first, slots_last,
-    load_sem, send_sem, recv_sem, wind_sem, out_sem,
+    wind_ref, owner_ref, active_ref, rate_tab, wind_tab, heat_tab,
+    load_sem, small_sem, send_sem, recv_sem, wind_sem, out_sem,
 ):
     cell_rows, cell_cols = fuel.shape
     refine = cell_rows // atm_rows
@@ -59,6 +60,15 @@
     ]
     load_fuel = pltpu.make_async_copy(fuel_ref, fuel, load_sem.at[cols])
     outer, inner = (0, cols - 1), tuple(range(1, cols - 1))
+    small = [
+        pltpu.make_async_copy(source, target, small_sem.at[i])
+        for i, (source, target) in enumerate((
+            (wind_any, wind_ref), (owner_any, owner_ref), (active_any, active_ref),
+            (rate_any, rate_tab), (drift_any, wind_tab), (heat_any, heat_tab),
+        ))
+    ]
+    for copy in small:
+        copy.start()
     for c in outer + inner:
         load_level[c].start()
     load_fuel.start()
@@ -160,28 +170,6 @@
         east_pack = jnp.where(lane == k, pltpu.roll(last, k + 1, 1), east_pack)
         return west_pack, east_pack
 
-    blank = jnp.zeros((atm_rows, LANES - atm_cols), F32)
-    mine = [jnp.concatenate([wind_ref[i], blank], axis=1) for i in range(2)]
-    packed_wind = pack(mine[0], mine[1])
-    for c in outer:
-        load_level[c].wait()
-
-    def first_columns(i, packs):
-        for q in range(tiles_in):
-            k = i * tiles_in + q
-            rows = pl.ds(pl.multiple_of(ROWS + k * ROWS, ROWS), ROWS)
-            packs = columns_into(packs, k, lev_a[0, rows, :], lev_a[cols - 1, rows, :])
-        return packs
-
-    empty = jnp.zeros((ROWS, LANES), F32)
-    packs = lax.fori_loop(0, groups, first_columns, (empty, empty))
-    pl.semaphore_wait(barrier, tiles - 1 + (g > 0).astype(jnp.int32) + (g < grps - 1).astype(jnp.int32))
-    share(packed_wind, wind_first, slots_first, 0)
-    start_columns(0, *packs)
-    for c in inner:
-        load_level[c].wait()
-    start_rows(0, lev_a)
-
     index = lax.broadcasted_iota(jnp.int32, spread.shape, 0) * refine
     place = lax.broadcasted_iota(jnp.int32, spread.shape, 1)
     spread[...] = jnp.where((place >= index) & (place < index + refine), 1.0, 0.0).astype(BF16)
@@ -195,7 +183,27 @@
             values = jnp.where(lane == category, ref[category], values)
         return values
 
+    for copy in small:
+        copy.wait()
     tables = [table(ref) for ref in (rate_tab, wind_tab, heat_tab)]
+    blank = jnp.zeros((atm_rows, LANES - atm_cols), F32)
+    mine = [jnp.concatenate([wind_ref[i], blank], axis=1) for i in range(2)]
+    packed_wind = pack(mine[0], mine[1])
+
+    pl.semaphore_wait(barrier, tiles - 1 + (g > 0).astype(jnp.int32) + (g < grps - 1).astype(jnp.int32))
+    share(packed_wind, wind_first, slots_first, 0)
+    empty = jnp.zeros((ROWS, LANES), F32)
+    packs = (empty, empty)
+    for c in outer:
+        load_level[c].wait()
+    for k in range(cell_rows // ROWS):
+        rows = pl.ds(ROWS + k * ROWS, ROWS)
+        packs = columns_into(packs, k, lev_a[0, rows, :], lev_a[cols - 1, rows, :])
+    start_columns(0, *packs)
+    for c in inner:
+        load_level[c].wait()
+    start_rows(0, lev_a)
+
     load_fuel.wait()
 
     def prepare(i, carry):
@@ -210,7 +218,7 @@
                 burn[rows, at] = jnp.tanh(lev_a[c, pl.ds(pl.multiple_of(start + ROWS, ROWS), ROWS), :])
         return carry
 
-    lax.fori_loop(0, groups, prepare, 0)
+    lax.fori_loop(0, groups, prepare, 0, unroll=2)
 
     def expand(east, north):
         wide = exact_dots([east, north], spread[...])
@@ -224,7 +232,7 @@
 
     def block(i, k, src, dst, want, packs):
         flux = k % SUBSTEPS == SUBSTEPS - 1
-        burning = jnp.where(active_ref[k, 0, 0] > 0, F32(1.0), F32(0.0))
+        burning = jnp.where(active_ref[k] > 0, F32(1.0), F32(0.0))
         ends = 0 in want
         if ends:
             west_halo, east_halo = halo[k, 0], halo[k, 1]
@@ -290,8 +298,14 @@
         if flux:
             for c in want:
                 for a in range(2):
-                    row_sums[c, pl.ds(2 * i + a, 1), :] = jnp.sum(sums[c][a], axis=0, keepdims=True)
+                    row_sums[c, pl.ds(pl.multiple_of((2 * i + a) * ROWS, ROWS), ROWS), :] = sums[c][a]
         return packs
+
+    def total_rows(c):
+        parts = [row_sums[c, pl.ds(s, atm_rows, stride=ROWS), :] for s in range(ROWS)]
+        while len(parts) > 1:
+            parts = [one + two for one, two in zip(parts[::2], parts[1::2])]
+        return parts[0]
 
     buffers = (lev_a, lev_b)
     store_level = [
@@ -304,7 +318,7 @@
         src, dst = buffers[k % 2], buffers[(k + 1) % 2]
         wait_sides(k)
         place_rows(k, src)
-        packs = lax.fori_loop(0, groups, lambda i, p: block(i, k, src, dst, outer, p), (empty, empty))
+        packs = lax.fori_loop(0, groups, lambda i, p: block(i, k, src, dst, outer, p), (empty, empty), unroll=2)
         if k < SUBS - 1:
             start_columns(k + 1, *packs)
         else:
@@ -315,15 +329,15 @@
             block(i, k, src, dst, inner, None)
             return carry
 
-        lax.fori_loop(0, 2, lambda n, carry: middle(n * (groups - 1), carry), 0)
+        lax.fori_loop(0, 2, lambda n, carry: middle(n * (groups - 1), carry), 0, unroll=2)
         if k < SUBS - 1:
             start_rows(k + 1, dst)
-        lax.fori_loop(1, groups - 1, middle, 0)
+        lax.fori_loop(1, groups - 1, middle, 0, unroll=2)
         if k == SUBS - 1:
             for c in inner:
                 store_level[c].start()
         if k % SUBSTEPS == SUBSTEPS - 1:
-            coarse = exact_dots([jnp.concatenate([row_sums[c] for c in range(cols)], axis=1)], gather_cols[...])[0] * F32(0.5 / (refine * refine))
+            coarse = exact_dots([jnp.concatenate([total_rows(c) for c in range(cols)], axis=1)], gather_cols[...])[0] * F32(0.5 / (refine * refine))
             west = jnp.where(lane16 == 0, coarse, pltpu.roll(coarse, 1, 1))
             east_c = jnp.where(lane16 == atm_cols - 1, coarse, pltpu.roll(coarse, LANES - 1, 1))
             up = jnp.where(sub16 == 0, coarse, pltpu.roll(coarse, 1, 0))
@@ -359,18 +373,18 @@
     cols = cell_cols // LANES
     padded = pltpu.VMEM((cols, cell_rows + 2 * ROWS, LANES), F32)
     tile = (ROWS, LANES)
-    vmem, smem = pl.BlockSpec(memory_space=pltpu.VMEM), pl.BlockSpec(memory_space=pltpu.SMEM)
+    vmem = pl.BlockSpec(memory_space=pltpu.VMEM)
     anywhere = pl.BlockSpec(memory_space=pl.ANY)
     return pl.pallas_call(
         functools.partial(kernel, grps, tiles, atm_rows, atm_cols),
         out_shape=(jax.ShapeDtypeStruct(level_set.shape, F32), jax.ShapeDtypeStruct(wind.shape, F32)),
-        in_specs=[anywhere, anywhere, vmem, smem, smem, smem, smem, smem],
+        in_specs=[anywhere] * 8,
         out_specs=(anywhere, vmem),
         scratch_shapes=[
             padded, padded,
             pltpu.VMEM((cell_rows, cell_cols), jnp.int32),
             cells, cells, cells, cells,
-            pltpu.VMEM((cols, atm_rows, LANES), F32),
+            pltpu.VMEM((cols, atm_rows * ROWS, LANES), F32),
             pltpu.VMEM((2, cols, atm_rows, LANES), F32),
             pltpu.VMEM((LANES, cell_cols), BF16),
             pltpu.VMEM((cell_cols, LANES), BF16),
@@ -380,16 +394,23 @@
             pltpu.VMEM(tile, F32),
             pltpu.VMEM((tiles,) + tile, F32),
             pltpu.VMEM((tiles,) + tile, F32),
+            pltpu.VMEM(wind.shape, F32),
+            pltpu.SMEM(owner.shape, jnp.int32),
+            pltpu.SMEM((SUBS,), jnp.int32),
+            pltpu.SMEM(fuel_rate.shape, F32),
+            pltpu.SMEM(fuel_wind.shape, F32),
+            pltpu.SMEM(fuel_heat.shape, F32),
             pltpu.SemaphoreType.DMA((cols + 1,)),
+            pltpu.SemaphoreType.DMA((6,)),
             pltpu.SemaphoreType.DMA((SUBS, 4)),
             pltpu.SemaphoreType.DMA((SUBS, 4)),
             pltpu.SemaphoreType.DMA((4,)),
             pltpu.SemaphoreType.DMA((cols,)),
         ],
         compiler_params=pltpu.CompilerParams(
-            collective_id=0, has_side_effects=True, vmem_limit_bytes=32 * 1024 * 1024
+            collective_id=0, has_side_effects=True, vmem_limit_bytes=60 * 1024 * 1024
         ),
-    )(level_set, fuel, wind, owner, active, fuel_rate, fuel_wind, fuel_heat)
+    )(level_set, fuel, wind, owner, active.reshape(SUBS), fuel_rate, fuel_wind, fuel_heat)
 
 
 def solution(mesh):

time: 38.8 us -> 33.1 us (0.85)
  Pallas kernels: 32.5 us -> 29.5 us
  local copies, waits for them, and re-layouts: 5.28 us -> 2.7 us
    pallas_call x1, Pallas kernels: 32.5 us -> 29.5 us  [shards(): pl.pallas_call(functools.partial(kernel, grps, tiles, atm_rows, atm_cols)...]
    unnamed x17 -> x4, local copies, waits for them, and re-layouts: 5.28 us -> 2.7 us
where the time goes in v2:
time: 33.1 us; the launch traced here: 32.8 us
  Pallas kernels  29.5 us (89%)
  local copies, waits for them, and re-layouts  2.7 us (8%)
  between operations  0.65 us (2%)
    pallas_call x1, Pallas kernels, shards(): pl.pallas_call(functools.partial(kernel, grps, tiles, atm_rows, atm_cols)...  29.5 us
    unnamed x4, local copies, waits for them, and re-layouts  2.7 us

profile of v2, /device:TPU:0, one launch (start us, length us, event | category | flops | bytes accessed | tf_op | source)
XLA Modules:
  0.0 32.8 jit_solution(172551401867913622)
XLA Ops:
  0.6 29.5 %shard_map.95 = (f32[320,640]{1,0:T(8,128)}, f32[2,16,32]{2,1,0:T(8,128)}) custom-call(f32[320,640]{1,0:T(8,128)} %level_ref.1, s32[320,640]{1,0:T(8,128)} %fuel_ref.1, f32[2,16,32]{2,1,0:T(8,128)} %wind_any.1, s32[1,16]{1,0:T(1,128)} %owner_any.1, s32[4]{0:T(128)} %bitcast.1, f32[13]{0:T(128)} %rate_any.1, f32[13]{0:T(128)} %drift_any.1, f32[13]{0:T(128)} %heat_any.1), custom_call_target="tpu_custom_call" | custom-call | tf_op jit(solution)/shard_map/pallas_call | solution.py:378
  30.1 0.0 copy-start
  30.1 2.1 %copy.12 = f32[320,640]{1,0:T(8,128)} copy(f32[320,640]{1,0:T(8,128)} %get-tuple-element.4) | data formatting | bytes 1638400
  32.2 0.0 copy-done
  32.2 0.6 %copy.13 = f32[2,16,32]{2,1,0:T(8,128)} copy(f32[2,16,32]{2,1,0:T(8,128)S(1)} %copy-done) | data formatting | bytes 8192
Async XLA Ops:
  30.1 2.1 %copy-start = (f32[2,16,32]{2,1,0:T(8,128)S(1)}, f32[2,16,32]{2,1,0:T(8,128)}, u32[]{:S(2)}) copy-start(f32[2,16,32]{2,1,0:T(8,128)} %get-tuple-element.5) | copy-start | bytes 12292

commit v3 on v2

--- a/solution.py
+++ b/solution.py
@@ -12,6 +12,7 @@
 SUBS = STEPS * SUBSTEPS
 MESH = pl.DeviceIdType.MESH
 LANES = 128
+PARTS = 8
 ROWS = 8
 F32 = jnp.float32
 BF16 = jnp.bfloat16
@@ -51,6 +52,18 @@
     tiles_in = group // ROWS
     groups = cell_rows // group
     g, t = lax.axis_index("grp"), lax.axis_index("tile")
+
+    barrier = pltpu.get_barrier_semaphore()
+    for d in range(1, tiles):
+        pl.semaphore_signal(barrier, inc=1, device_id=(g, lax.rem(t + d, tiles)), device_id_type=MESH)
+
+    @pl.when(g > 0)
+    def _():
+        pl.semaphore_signal(barrier, inc=1, device_id=(g - 1, t), device_id_type=MESH)
+
+    @pl.when(g < grps - 1)
+    def _():
+        pl.semaphore_signal(barrier, inc=1, device_id=(g + 1, t), device_id_type=MESH)
 
     load_level = [
         pltpu.make_async_copy(
@@ -72,18 +85,6 @@
     for c in outer + inner:
         load_level[c].start()
     load_fuel.start()
-
-    barrier = pltpu.get_barrier_semaphore()
-    for d in range(1, tiles):
-        pl.semaphore_signal(barrier, inc=1, device_id=(g, lax.rem(t + d, tiles)), device_id_type=MESH)
-
-    @pl.when(g > 0)
-    def _():
-        pl.semaphore_signal(barrier, inc=1, device_id=(g - 1, t), device_id_type=MESH)
-
-    @pl.when(g < grps - 1)
-    def _():
-        pl.semaphore_signal(barrier, inc=1, device_id=(g + 1, t), device_id_type=MESH)
 
     lane = lax.broadcasted_iota(jnp.int32, (ROWS, LANES), 1)
     sub = lax.broadcasted_iota(jnp.int32, (ROWS, LANES), 0)
@@ -366,6 +367,18 @@
                 halo_copy(k, side, targets[side]).wait_send()
 
 
+def hand_out(level, held, level_out, wind_out, sem):
+    rows = level.shape[0] // PARTS
+    copies = [pltpu.make_async_copy(held, wind_out, sem.at[PARTS])]
+    for i in range(PARTS):
+        part = pl.ds(i * rows, rows)
+        copies.append(pltpu.make_async_copy(level.at[part, :], level_out.at[part, :], sem.at[i]))
+    for copy in copies:
+        copy.start()
+    for copy in copies:
+        copy.wait()
+
+
 def shards(grps, tiles, level_set, fuel, wind, owner, active, fuel_rate, fuel_wind, fuel_heat):
     cell_rows, cell_cols = level_set.shape
     atm_rows, atm_cols = wind.shape[1], wind.shape[2]
@@ -375,7 +388,7 @@
     tile = (ROWS, LANES)
     vmem = pl.BlockSpec(memory_space=pltpu.VMEM)
     anywhere = pl.BlockSpec(memory_space=pl.ANY)
-    return pl.pallas_call(
+    level, held = pl.pallas_call(
         functools.partial(kernel, grps, tiles, atm_rows, atm_cols),
         out_shape=(jax.ShapeDtypeStruct(level_set.shape, F32), jax.ShapeDtypeStruct(wind.shape, F32)),
         in_specs=[anywhere] * 8,
@@ -412,6 +425,15 @@
         ),
     )(level_set, fuel, wind, owner, active.reshape(SUBS), fuel_rate, fuel_wind, fuel_heat)
 
+    return pl.pallas_call(
+        hand_out,
+        out_shape=(jax.ShapeDtypeStruct(level_set.shape, F32), jax.ShapeDtypeStruct(wind.shape, F32)),
+        in_specs=[anywhere] * 2,
+        out_specs=(anywhere, anywhere),
+        scratch_shapes=[pltpu.SemaphoreType.DMA((PARTS + 1,))],
+        compiler_params=pltpu.CompilerParams(vmem_limit_bytes=60 * 1024 * 1024),
+    )(level, held)
+
 
 def solution(mesh):
     in_specs = (

time: 33.1 us -> 56.9 us (1.72)
  Pallas kernels: 29.5 us -> 56 us
  local copies, waits for them, and re-layouts: 2.7 us -> 0 us
    pallas_call x0 -> x1, Pallas kernels: none -> 26.5 us  [shards(): pl.pallas_call(hand_out, out_shape=(jax.ShapeDtypeStruct(level_set.shape,...]
    unnamed x4 -> x0, local copies, waits for them, and re-layouts: 2.7 us -> none
where the time goes in v3:
time: 56.9 us; the launch traced here: 56.6 us
  Pallas kernels  56 us (98%)
  between operations  0.64 us (1%)
    pallas_call x1, Pallas kernels, shards(): pl.pallas_call(functools.partial(kernel, grps, tiles, atm_rows, atm_cols)...  29.5 us
    pallas_call x1, Pallas kernels, shards(): pl.pallas_call(hand_out, out_shape=(jax.ShapeDtypeStruct(level_set.shape,...  26.5 us

profile of v3, /device:TPU:0, one launch (start us, length us, event | category | flops | bytes accessed | tf_op | source)
XLA Modules:
  0.0 56.6 jit_solution(12954755418375397825)
XLA Ops:
  0.6 29.5 %shard_map.95 = (f32[320,640]{1,0:T(8,128)}, f32[2,16,32]{2,1,0:T(8,128)}) custom-call(f32[320,640]{1,0:T(8,128)} %level_ref.1, s32[320,640]{1,0:T(8,128)} %fuel_ref.1, f32[2,16,32]{2,1,0:T(8,128)} %wind_any.1, s32[1,16]{1,0:T(1,128)} %owner_any.1, s32[4]{0:T(128)} %bitcast.1, f32[13]{0:T(128)} %rate_any.1, f32[13]{0:T(128)} %drift_any.1, f32[13]{0:T(128)} %heat_any.1), custom_call_target="tpu_custom_call" | custom-call | tf_op jit(solution)/shard_map/pallas_call | solution.py:391
  30.1 26.5 %shard_map.96 = (f32[320,640]{1,0:T(8,128)}, f32[2,16,32]{2,1,0:T(8,128)}) custom-call(f32[320,640]{1,0:T(8,128)} %get-tuple-element.4.level, f32[2,16,32]{2,1,0:T(8,128)} %get-tuple-element.5.held), custom_call_target="tpu_custom_call" | custom-call | tf_op jit(solution)/shard_map/pallas_call | solution.py:428

commit v4 on v3

--- a/solution.py
+++ b/solution.py
@@ -12,7 +12,7 @@
 SUBS = STEPS * SUBSTEPS
 MESH = pl.DeviceIdType.MESH
 LANES = 128
-PARTS = 8
+PARTS = 4
 ROWS = 8
 F32 = jnp.float32
 BF16 = jnp.bfloat16
@@ -367,15 +367,20 @@
                 halo_copy(k, side, targets[side]).wait_send()
 
 
-def hand_out(level, held, level_out, wind_out, sem):
+def hand_out(level, held, level_out, wind_out, level_held, wind_held, in_sem, out_sem):
     rows = level.shape[0] // PARTS
-    copies = [pltpu.make_async_copy(held, wind_out, sem.at[PARTS])]
+    views = [(held, wind_held, wind_out)]
     for i in range(PARTS):
         part = pl.ds(i * rows, rows)
-        copies.append(pltpu.make_async_copy(level.at[part, :], level_out.at[part, :], sem.at[i]))
-    for copy in copies:
+        views.append(tuple(ref.at[part, :] for ref in (level, level_held, level_out)))
+    inward = [pltpu.make_async_copy(a, b, in_sem.at[i]) for i, (a, b, _) in enumerate(views)]
+    outward = [pltpu.make_async_copy(b, c, out_sem.at[i]) for i, (_, b, c) in enumerate(views)]
+    for copy in inward:
         copy.start()
-    for copy in copies:
+    for first, second in zip(inward, outward):
+        first.wait()
+        second.start()
+    for copy in outward:
         copy.wait()
 
 
@@ -430,7 +435,10 @@
         out_shape=(jax.ShapeDtypeStruct(level_set.shape, F32), jax.ShapeDtypeStruct(wind.shape, F32)),
         in_specs=[anywhere] * 2,
         out_specs=(anywhere, anywhere),
-        scratch_shapes=[pltpu.SemaphoreType.DMA((PARTS + 1,))],
+        scratch_shapes=[
+            pltpu.VMEM(level_set.shape, F32), pltpu.VMEM(wind.shape, F32),
+            pltpu.SemaphoreType.DMA((PARTS + 1,)), pltpu.SemaphoreType.DMA((PARTS + 1,)),
+        ],
         compiler_params=pltpu.CompilerParams(vmem_limit_bytes=60 * 1024 * 1024),
     )(level, held)
 

time: 56.9 us -> 32.5 us (0.57)
  Pallas kernels: 56 us -> 31.5 us
    pallas_call x1, Pallas kernels: 26.5 us -> 2.01 us  [shards(): pl.pallas_call(hand_out, out_shape=(jax.ShapeDtypeStruct(level_set.shape,...]
where the time goes in v4:
time: 32.5 us; the launch traced here: 32.1 us
  Pallas kernels  31.5 us (97%)
  between operations  0.64 us (2%)
    pallas_call x1, Pallas kernels, shards(): pl.pallas_call(functools.partial(kernel, grps, tiles, atm_rows, atm_cols)...  29.5 us
    pallas_call x1, Pallas kernels, shards(): pl.pallas_call(hand_out, out_shape=(jax.ShapeDtypeStruct(level_set.shape,...  2.01 us

profile of v4, /device:TPU:0, one launch (start us, length us, event | category | flops | bytes accessed | tf_op | source)
XLA Modules:
  0.0 32.1 jit_solution(17665655309679819799)
XLA Ops:
  0.6 29.5 %shard_map.95 = (f32[320,640]{1,0:T(8,128)}, f32[2,16,32]{2,1,0:T(8,128)}) custom-call(f32[320,640]{1,0:T(8,128)} %level_ref.1, s32[320,640]{1,0:T(8,128)} %fuel_ref.1, f32[2,16,32]{2,1,0:T(8,128)} %wind_any.1, s32[1,16]{1,0:T(1,128)} %owner_any.1, s32[4]{0:T(128)} %bitcast.1, f32[13]{0:T(128)} %rate_any.1, f32[13]{0:T(128)} %drift_any.1, f32[13]{0:T(128)} %heat_any.1), custom_call_target="tpu_custom_call" | custom-call | tf_op jit(solution)/shard_map/pallas_call | solution.py:396
  30.1 2.0 %shard_map.96 = (f32[320,640]{1,0:T(8,128)}, f32[2,16,32]{2,1,0:T(8,128)}) custom-call(f32[320,640]{1,0:T(8,128)} %get-tuple-element.4.level, f32[2,16,32]{2,1,0:T(8,128)} %get-tuple-element.5.held), custom_call_target="tpu_custom_call" | custom-call | tf_op jit(solution)/shard_map/pallas_call | solution.py:433

commit v5 on v4

--- a/solution.py
+++ b/solution.py
@@ -184,9 +184,7 @@
             values = jnp.where(lane == category, ref[category], values)
         return values
 
-    for copy in small:
-        copy.wait()
-    tables = [table(ref) for ref in (rate_tab, wind_tab, heat_tab)]
+    small[0].wait()
     blank = jnp.zeros((atm_rows, LANES - atm_cols), F32)
     mine = [jnp.concatenate([wind_ref[i], blank], axis=1) for i in range(2)]
     packed_wind = pack(mine[0], mine[1])
@@ -205,6 +203,9 @@
         load_level[c].wait()
     start_rows(0, lev_a)
 
+    for copy in small[1:]:
+        copy.wait()
+    tables = [table(ref) for ref in (rate_tab, wind_tab, heat_tab)]
     load_fuel.wait()
 
     def prepare(i, carry):
@@ -333,7 +334,7 @@
         lax.fori_loop(0, 2, lambda n, carry: middle(n * (groups - 1), carry), 0, unroll=2)
         if k < SUBS - 1:
             start_rows(k + 1, dst)
-        lax.fori_loop(1, groups - 1, middle, 0, unroll=2)
+        lax.fori_loop(1, groups - 1, middle, 0, unroll=3)
         if k == SUBS - 1:
             for c in inner:
                 store_level[c].start()

time: 32.5 us -> 32.4 us (level)
  no operation moved by 1% of the time
where the time goes in v5:
time: 32.4 us; the launch traced here: 32.1 us
  Pallas kernels  31.4 us (97%)
  between operations  0.64 us (2%)
    pallas_call x1, Pallas kernels, shards(): pl.pallas_call(functools.partial(kernel, grps, tiles, atm_rows, atm_cols)...  29.4 us
    pallas_call x1, Pallas kernels, shards(): pl.pallas_call(hand_out, out_shape=(jax.ShapeDtypeStruct(level_set.shape,...  2.01 us

profile of v5, /device:TPU:0, one launch (start us, length us, event | category | flops | bytes accessed | tf_op | source)
XLA Modules:
  0.0 32.1 jit_solution(14885500402919337341)
XLA Ops:
  0.6 29.4 %shard_map.95 = (f32[320,640]{1,0:T(8,128)}, f32[2,16,32]{2,1,0:T(8,128)}) custom-call(f32[320,640]{1,0:T(8,128)} %level_ref.1, s32[320,640]{1,0:T(8,128)} %fuel_ref.1, f32[2,16,32]{2,1,0:T(8,128)} %wind_any.1, s32[1,16]{1,0:T(1,128)} %owner_any.1, s32[4]{0:T(128)} %bitcast.1, f32[13]{0:T(128)} %rate_any.1, f32[13]{0:T(128)} %drift_any.1, f32[13]{0:T(128)} %heat_any.1), custom_call_target="tpu_custom_call" | custom-call | tf_op jit(solution)/shard_map/pallas_call | solution.py:397
  30.1 2.0 %shard_map.96 = (f32[320,640]{1,0:T(8,128)}, f32[2,16,32]{2,1,0:T(8,128)}) custom-call(f32[320,640]{1,0:T(8,128)} %get-tuple-element.4.level, f32[2,16,32]{2,1,0:T(8,128)} %get-tuple-element.5.held), custom_call_target="tpu_custom_call" | custom-call | tf_op jit(solution)/shard_map/pallas_call | solution.py:434
